TPU v7x, 128 devices: a whole 4x4x4 slice. The times are simulated.
128 devices in a mesh: section: 16 (over x, z_hi, core), tp: 8 (over y, z_lo).
Axes of the slice: x: 4, y: 4, z: 4 (z_hi: 2, z_lo: 2; z = z_hi * 2 + z_lo), core: 2. Of those that a mesh axis runs over, the one named last changes fastest.
Arguments:
- fresh_input: bfloat16 [1024, 3072], P(None, 'tp'), may hold values from -80 to 80
- previous_out: bfloat16 [16384, 3072], P('section', 'tp'), may hold values from -80 to 80
- norm_gain: bfloat16 [16, 3072], P('section', 'tp'), may hold values from 0.099609375 to 1.8984375
- gate_weight: bfloat16 [16, 3072, 8192], P('section', None, 'tp'), may hold values from -0.109375 to 0.109375
- up_weight: bfloat16 [16, 3072, 8192], P('section', None, 'tp'), may hold values from -0.109375 to 0.109375
- down_weight: bfloat16 [16, 8192, 3072], P('section', 'tp'), may hold values from -0.25 to 0.25
Outputs:
- section_out: bfloat16 [16384, 3072], P('section', 'tp')
All inputs are finite; a program needn't handle non-finite values.
Results may differ from a plain program's by a relative error of at most 0.015.
Values may be sent and summed in bfloat16 or wider, within the bound.
A program may use at most 128 MiB of HBM per device.

v0:
```python
import math

import jax
import jax.numpy as jnp
from jax import lax
from jax.sharding import PartitionSpec as P

EPSILON = 1e-05
BLOCK_EPSILON = 1e-06
CLIP_FACTOR = 2.0


def from_behind(array, axis, by):
    size = lax.axis_size(axis)
    pairs = [(i, i + by) for i in range(size) if 0 <= i + by < size]
    return lax.ppermute(array, axis, pairs)


def hadamard_table():
    indices = jnp.arange(128, dtype=jnp.int32)
    intersection = indices[:, None] & indices[None, :]
    parity = jnp.zeros_like(intersection)
    for bit_pos in range(7):
        parity = parity + (intersection >> bit_pos & 1)
    sign_table = 1 - 2 * (parity % 2)
    return sign_table.astype(jnp.float32) / math.sqrt(128.0)


def rotate(values, hadamard):
    dims_now = values.shape
    blocks = values.reshape(dims_now[:-1] + (dims_now[-1] // 128, 128))
    turned = jnp.einsum("...k,kj->...j", blocks, hadamard, precision=lax.Precision.HIGHEST)
    return turned.reshape(dims_now)


def saturate(values):
    dims_now = values.shape
    blocks = values.reshape(dims_now[:-1] + (dims_now[-1] // 128, 128))
    limit = CLIP_FACTOR * jnp.sqrt(
        jnp.mean(blocks * blocks, axis=-1, keepdims=True) + BLOCK_EPSILON
    )
    return jnp.clip(blocks, -limit, limit).reshape(dims_now)


def local(fresh_input, previous_out, norm_gain, gate_weight, up_weight, down_weight):
    hadamard = hadamard_table()
    shifted = from_behind(previous_out, "section", 1)
    is_first = lax.axis_index("section") == 0
    current = jnp.where(is_first, fresh_input, shifted)
    wide_part = current.astype(jnp.float32)
    whole_rows, whole_gain = (
        lax.all_gather(current, "tp", axis=1, tiled=True),
        lax.all_gather(norm_gain, "tp", axis=1, tiled=True),
    )
    wide_rows = whole_rows.astype(jnp.float32)
    mean_square = jnp.mean(wide_rows * wide_rows, axis=1, keepdims=True)
    normed = (
        wide_rows * lax.rsqrt(mean_square + EPSILON) * whole_gain[0].astype(jnp.float32)[None, :]
    ).astype(jnp.bfloat16)
    gate_out = jnp.dot(normed, gate_weight[0], preferred_element_type=jnp.float32)
    up_out = jnp.dot(normed, up_weight[0], preferred_element_type=jnp.float32)
    hidden = (jax.nn.silu(gate_out) * up_out).astype(jnp.bfloat16)
    term_full = jnp.dot(hidden, down_weight[0], preferred_element_type=jnp.float32)
    rotated = saturate(rotate(term_full, hadamard))
    part_width = current.shape[1]
    summed_all = lax.psum(rotated.astype(jnp.bfloat16), "tp").astype(jnp.float32)
    total_sum = lax.dynamic_slice_in_dim(
        summed_all, lax.axis_index("tp") * part_width, part_width, 1
    )
    update = rotate(total_sum, hadamard)
    return (wide_part + update).astype(jnp.bfloat16)


def solution(mesh):
    in_specs = (
        P(None, "tp"),
        P("section", "tp"),
        P("section", "tp"),
        P("section", None, "tp"),
        P("section", None, "tp"),
        P("section", "tp", None),
    )
    out_specs = P("section", "tp")
    return jax.shard_map(local, mesh=mesh, in_specs=in_specs, out_specs=out_specs, check_vma=False)
```

profile of v0, /device:TPU:0, one launch (start us, length us, event | category | flops | bytes accessed | tf_op | source)
XLA Modules:
  0.0 489.0 jit_solution(13272611002683223128)
XLA Ops:
  6.5 0.0 all-gather.2.cloned.1.call-start
  6.5 1.3 collective-permute-start
  7.9 2.0 collective-permute-done
  9.9 2.1 broadcast_select_fusion
  12.0 0.0 all-gather.2.cloned.1.call-update
  12.1 0.0 all-reduce.2.cloned.1.call-start
  12.1 24.9 %all_gather.7 = bf16[1,3072]{1,0:T(2,128)(2,1)S(1)} all-gather(bf16[1,384]{1,0:T(2,128)(2,1)} %param.8), channel_id=1, replica_groups=mesh['section'=16,'tp'=8] {'tp'}, dimensions={1}, use_global_device_ids=true | all-gather | bytes 6912 | tf_op jit(solution)/shard_map/all_gather | solution.py:53
  37.0 117.3 %all-gather.2.cloned.1.call-done = bf16[1024,3072]{1,0:T(8,128)(2,1)} async-done(((bf16[1024,384]{1,0:T(8,128)(2,1)}), bf16[1024,3072]{1,0:T(8,128)(2,1)}) %all-gather.2.cloned.1.call-update) | async-done | bytes 6291472 | tf_op jit(solution)/shard_map/all_gather | solution.py:52
  154.4 0.0 copy-start.1
  154.4 0.0 slice-start
  154.4 4.2 fusion
  158.6 0.4 copy-done.1
  159.0 0.0 slice-start.1
  159.0 0.0 slice-start.2
  159.0 9.0 %fusion.6 = f32[1024,1024]{1,0:T(8,128)S(1)} fusion(bf16[1,3072,1024]{2,1,0:T(8,128)(2,1)} %param.10, bf16[1024,3072]{1,0:T(8,128)(2,1)S(1)} %copy-done.1, f32[3072]{0:T(1024)S(1)} %bitcast.34, f32[1024]{0:T(1024)S(1)} %add_rsqrt_fusion), kind=kOutput, calls=%fused_computation.10 | convolution fusion | flops 6455033856 | bytes 16793600 | tf_op jit(solution)/shard_map/dot_general | solution.py:61
  168.0 0.0 slice-done
  168.0 0.0 slice-done.1
  168.0 0.0 slice-start.3
  168.1 8.5 %fusion.8 = f32[1024,1024]{1,0:T(8,128)} fusion(bf16[1,3072,1024]{2,1,0:T(8,128)(2,1)S(1)} %bitcast.37, bf16[1024,3072]{1,0:T(8,128)(2,1)S(1)} %copy-done.1, f32[3072]{0:T(1024)S(1)} %bitcast.35, f32[1024]{0:T(1024)S(1)} %add_rsqrt_fusion), kind=kOutput, calls=%fused_computation.12 | convolution fusion | flops 6455033856 | bytes 16793600 | tf_op jit(solution)/shard_map/dot_general | solution.py:60
  176.6 0.0 slice-done.2
  176.6 0.0 slice-done.3
  176.6 11.5 %fusion.3 = f32[1024,24,128]{2,0,1:T(8,128)} fusion(f32[1024,1024]{1,0:T(8,128)S(1)} %fusion.6, f32[1024,1024]{1,0:T(8,128)} %fusion.8, bf16[1,1024,3072]{2,1,0:T(8,128)(2,1)S(1)} %bitcast.39), kind=kOutput, calls=%fused_computation.7 | convolution fusion | flops 6448742400 | bytes 27262976 | tf_op jit(solution)/shard_map/dot_general | solution.py:63
  188.1 15.6 %multiply_reduce_fusion = (f32[1024,24]{0,1:T(8,128)S(1)}, bf16[1024,24,128]{0,2,1:T(8,128)(2,1)S(1)}) fusion(f32[1024,24,128]{2,0,1:T(8,128)} %fusion.3), kind=kOutput, calls=%fused_computation.6 | convolution fusion | flops 4841840640 | bytes 18972672 | tf_op jit(solution)/shard_map/...k,kj->...j/dot_general | solution.py:32
  203.8 3.2 minimum_convert_fusion
  206.9 0.0 copy-start
  206.9 0.0 all-reduce.2.cloned.1.call-update
  207.0 269.0 %all-reduce.2.cloned.1.call-done = bf16[1024,3072]{0,1:T(8,128)(2,1)} async-done(((bf16[1024,3072]{0,1:T(8,128)(2,1)}), bf16[1024,3072]{0,1:T(8,128)(2,1)}) %all-reduce.2.cloned.1.call-update) | async-done | bytes 6291472 | tf_op jit(solution)/shard_map/psum | solution.py:66
  476.0 1.2 constant_dynamic-slice_fusion
  477.2 2.0 fusion.19
  479.2 1.9 copy.9
  481.1 0.0 copy-done
  481.1 1.0 add_convert_fusion
  (5 shorter events, 0.1 us)
Async XLA Ops:
  6.5 147.8 %all-gather.2.cloned.1.call-start = ((), (), s32[]{:S(2)}) async-start(), calls=%async_computation | async-start | bytes 7077888 | tf_op jit(solution)/shard_map/all_gather | solution.py:52
  6.5 3.4 collective-permute-start
  12.1 464.0 %all-reduce.2.cloned.1.call-start = ((), (), s32[]{:S(2)}) async-start(), calls=%async_computation.1 | async-start | bytes 12582912 | tf_op jit(solution)/shard_map/psum | solution.py:66
  154.4 4.6 copy-start.1
  154.4 13.6 %slice-start = ((s8[6291456]{0:T(1024)(128)(4,1)}), s8[2097152]{0:T(1024)(128)(4,1)S(1)}, s32[]{:S(2)}) async-start(s8[6291456]{0:T(1024)(128)(4,1)} %bitcast.36), calls=%async_computation.2 | async-start | bytes 4194304
  159.0 9.1 %slice-start.1 = ((s8[6291456]{0:T(1024)(128)(4,1)}), s8[4194304]{0:T(1024)(128)(4,1)S(1)}, s32[]{:S(2)}) async-start(s8[6291456]{0:T(1024)(128)(4,1)} %bitcast.36), calls=%async_computation.3 | async-start | bytes 8388608
  159.0 17.6 %slice-start.2 = ((s8[6291456]{0:T(1024)(128)(4,1)}), s8[4194304]{0:T(1024)(128)(4,1)S(1)}, s32[]{:S(2)}) async-start(s8[6291456]{0:T(1024)(128)(4,1)} %bitcast.38), calls=%async_computation.4 | async-start | bytes 8388608
  168.0 8.5 %slice-start.3 = ((s8[6291456]{0:T(1024)(128)(4,1)}), s8[2097152]{0:T(1024)(128)(4,1)S(1)}, s32[]{:S(2)}) async-start(s8[6291456]{0:T(1024)(128)(4,1)} %bitcast.38), calls=%async_computation.5 | async-start | bytes 4194304
  206.9 274.2 %copy-start = (bf16[1024,384]{1,0:T(8,128)(2,1)S(1)}, bf16[1024,384]{1,0:T(8,128)(2,1)}, u32[]{:S(2)}) copy-start(bf16[1024,384]{1,0:T(8,128)(2,1)} %broadcast_select_fusion) | copy-start | bytes 2359300
Sparse Core Ops, SparseCore 0:
  12.2 142.1 all-gather.1
  207.1 268.8 all-reduce.1
where the time goes:
time: 493 us; the launch traced here: 489 us
  waiting for transfers between devices  388 us (79%)
  matrix products  46.7 us (9%)
  blocking collectives  24.9 us (5%)
  between operations  13.5 us (3%)
  other arithmetic  10.6 us (2%)
    psum x1, waiting for transfers between devices, local(): lax.psum(rotated.astype(jnp.bfloat16), 'tp').astype(jnp.float32)  269 us
    all_gather x1, waiting for transfers between devices, local(): lax.all_gather(current, 'tp', axis=1, tiled=True)  117 us
    all_gather x1, blocking collectives, local(): lax.all_gather(norm_gain, 'tp', axis=1, tiled=True)  24.9 us
    dot_general x2, matrix products, rotate(): jnp.einsum('...k,kj->...j', blocks, hadamard, precision=lax.Precision.HIG...  17.6 us
    dot_general x1, matrix products, local(): jnp.dot(hidden, down_weight[0], preferred_element_type=jnp.float32)  11.5 us
  transfers between devices with their start and end apart: 3, of which 3 were waited for; matrix products, arithmetic and copies ran while one was open for 0% of the time, Pallas kernels for 0%

commit v1 on v0

v1 whole, which is shorter than its diff:
```python
import math

import jax
import jax.numpy as jnp
from jax import lax
from jax.experimental import pallas as pl
from jax.experimental.pallas import tpu as pltpu
from jax.sharding import PartitionSpec as P

EPSILON = 1e-05
BLOCK_EPSILON = 1e-06
CLIP_FACTOR = 2.0

MESH = pl.DeviceIdType.MESH
F32 = jnp.float32
BF16 = jnp.bfloat16

TOK = 1024
D = 3072
H_DEV = 1024
PART = 384
ROWS = 256
CHUNKS = TOK // ROWS
TILE = 256
COPIES = 30

LO, HALF, HI = 48, 128, 192


def kernel(
    fresh_ref, prev_ref, gain_ref, gate_ref, up_ref, down_ref, out_ref,
    xg, wg, wu, wd, rot, land1, land2, land3, nb, hb, gains, hada, ones,
    load_sem, fresh_sem, relay_send, relay_recv, gain_send, gain_recv, send, recv,
):
    s = lax.axis_index("section")
    t = lax.axis_index("tp")
    n_sections = lax.axis_size("section")
    n_tp = lax.axis_size("tp")
    y, z = t // 2, t % 2
    core = s % 2
    yp, ym, yf = (y + 1) % 4, (y + 3) % 4, (y + 2) % 4
    zb = 1 - z
    dev_p, dev_m, dev_z = (s, yp * 2 + z), (s, ym * 2 + z), (s, y * 2 + zb)
    has_next = s < n_sections - 1
    has_prev = s > 0
    next_dev = (jnp.minimum(s + 1, n_sections - 1), jnp.where(core == 0, t, y * 2 + zb))
    prev_dev = (jnp.maximum(s - 1, 0), jnp.where(core == 1, t, y * 2 + zb))
    zo = jnp.where(jnp.logical_or(core == 1, s == 0), z, zb)
    zq = 1 - zo

    loads = [
        pltpu.make_async_copy(src, dst, load_sem.at[i])
        for i, (src, dst) in enumerate(((down_ref.at[0], wd), (gate_ref.at[0], wg), (up_ref.at[0], wu)))
    ]
    for load in loads:
        load.start()

    barrier = pltpu.get_barrier_semaphore()
    for q in range(1, n_tp):
        pl.semaphore_signal(barrier, inc=1, device_id=(s, (t + q) % n_tp), device_id_type=MESH)

    @pl.when(has_next)
    def _():
        pl.semaphore_signal(barrier, inc=1, device_id=next_dev, device_id_type=MESH)

    @pl.when(has_prev)
    def _():
        pl.semaphore_signal(barrier, inc=1, device_id=prev_dev, device_id_type=MESH)

    pl.semaphore_wait(barrier, n_tp - 1 + has_next.astype(jnp.int32) + has_prev.astype(jnp.int32))

    def columns(yy, zz):
        return pl.ds(pl.multiple_of((yy * 2 + zz) * PART, 128), PART)

    def relay(c):
        return pltpu.make_async_remote_copy(
            prev_ref.at[pl.ds(pl.multiple_of(c * ROWS, ROWS), ROWS)],
            xg.at[c, :, columns(y, z)],
            relay_send.at[c],
            relay_recv.at[c],
            device_id=next_dev,
            device_id_type=MESH,
        )

    def fresh(c):
        return pltpu.make_async_copy(
            fresh_ref.at[pl.ds(pl.multiple_of(c * ROWS, ROWS), ROWS)],
            xg.at[c, :, columns(y, z)],
            fresh_sem.at[c],
        )

    @pl.when(has_next)
    def _():
        for c in range(CHUNKS):
            relay(c).start()

    @pl.when(s == 0)
    def _():
        for c in range(CHUNKS):
            fresh(c).start()

    def gain_copy(q):
        return pltpu.make_async_remote_copy(
            gains.at[:, columns(y, z)],
            gains.at[:, columns(y, z)],
            gain_send.at[q - 1],
            gain_recv.at[q - 1],
            device_id=(s, (t + q) % n_tp),
            device_id_type=MESH,
        )

    gains[:, columns(y, z)] = jnp.broadcast_to(gain_ref[...].astype(F32), (8, PART))
    for q in range(1, n_tp):
        gain_copy(q).start()

    row_id = lax.broadcasted_iota(jnp.int32, (TILE, TILE), 0)
    col_id = lax.broadcasted_iota(jnp.int32, (TILE, TILE), 1)
    common = (row_id & col_id) & 127
    parity = common
    for shift in (4, 2, 1):
        parity = parity ^ (parity >> shift)
    same = (row_id >> 7) == (col_id >> 7)
    hada[...] = jnp.where(same, (1 - 2 * (parity & 1)).astype(F32), 0.0).astype(BF16)
    ones[...] = jnp.where(same, 1.0, 0.0).astype(BF16)

    def x_at(c, low, high, yy, zz):
        return xg.at[c, pl.ds(low, high - low), columns(yy, zz)]

    def r_at(c, low, high, yy, zz):
        return rot.at[c, pl.ds(low, high - low), columns(yy, zz)]

    def gathered(c, k):
        low, high, yy, zz, dev = (
            (0, ROWS, y, zo, dev_z),
            (0, ROWS, y, zo, dev_p),
            (0, ROWS, y, zo, dev_m),
            (LO, HI, y, zq, dev_p),
            (LO, HI, y, zq, dev_m),
            (0, HALF, ym, zo, dev_p),
            (HALF, ROWS, yp, zo, dev_m),
            (0, LO, ym, zo, dev_z),
            (HI, ROWS, ym, zo, dev_z),
            (0, LO, yp, zo, dev_z),
            (HI, ROWS, yp, zo, dev_z),
            (0, LO, yf, zo, dev_z),
            (HI, ROWS, yf, zo, dev_z),
            (LO, HALF, ym, zq, dev_p),
            (HALF, HI, yp, zq, dev_m),
        )[k]
        ref = x_at(c, low, high, yy, zz)
        return ref, ref, dev

    def summed(c, k):
        low, high, yy, zz, dev, dst = (
            (0, LO, yf, zb, dev_z, land1.at[c, pl.ds(0, LO)]),
            (HI, ROWS, yf, zb, dev_z, land1.at[c, pl.ds(HI, ROWS - HI)]),
            (LO, HALF, yf, zb, dev_p, land1.at[c, pl.ds(LO, HALF - LO)]),
            (HALF, HI, yf, zb, dev_m, land1.at[c, pl.ds(HALF, HI - HALF)]),
            (0, HALF, yf, z, dev_p, land2.at[c, pl.ds(0, HALF)]),
            (HALF, ROWS, yf, z, dev_m, land2.at[c, pl.ds(HALF, ROWS - HALF)]),
            (LO, HI, yp, zb, dev_p, land2.at[c, pl.ds(256, HI - LO)]),
            (LO, HI, ym, zb, dev_m, land2.at[c, pl.ds(400, HI - LO)]),
            (0, LO, yp, zb, dev_z, land2.at[c, pl.ds(544, LO)]),
            (HI, ROWS, yp, zb, dev_z, land2.at[c, pl.ds(592, ROWS - HI)]),
            (0, LO, ym, zb, dev_z, land2.at[c, pl.ds(656, LO)]),
            (HI, ROWS, ym, zb, dev_z, land2.at[c, pl.ds(704, ROWS - HI)]),
            (0, ROWS, yp, z, dev_p, land3.at[c, 0]),
            (0, ROWS, ym, z, dev_m, land3.at[c, 1]),
            (0, ROWS, y, zb, dev_z, land3.at[c, 2]),
        )[k - 15]
        return r_at(c, low, high, yy, zz), dst, dev

    def copy(c, k):
        src, dst, dev = gathered(c, k) if k < 15 else summed(c, k)
        return pltpu.make_async_remote_copy(
            src, dst, send.at[c, k], recv.at[c, k], device_id=dev, device_id_type=MESH
        )

    def start(c, *ks):
        for k in ks:
            copy(c, k).start()

    def arrive(c, *ks):
        for k in ks:
            copy(c, k).wait_recv()

    def gather_one(c):
        @pl.when(s == 0)
        def _():
            fresh(c).wait()

        @pl.when(has_prev)
        def _():
            relay(c).wait_recv()

        start(c, 0, 1, 2)

    def gather_two(c):
        arrive(c, 1)
        start(c, 5, 7, 8)
        arrive(c, 2)
        start(c, 6, 9, 10)
        arrive(c, 0)
        start(c, 3, 4)

    def gather_three(c):
        arrive(c, 5)
        start(c, 11)
        arrive(c, 6)
        start(c, 12)
        arrive(c, 3)
        start(c, 13)
        arrive(c, 4)
        start(c, 14)

    def turn_weights(first, count):
        def body(i, carry):
            at = first * 4 + i
            rows = pl.ds(pl.multiple_of((at % 4) * 256, 256), 256)
            cols = pl.ds(pl.multiple_of((at // 4) * TILE, TILE), TILE)
            turned = jnp.dot(wd[rows, cols], hada[...], preferred_element_type=F32)
            wd[rows, cols] = (turned * (1.0 / math.sqrt(128.0))).astype(BF16)
            return carry

        lax.fori_loop(0, count * 4, body, 0)

    def compute(c):
        arrive(c, 7, 8, 9, 10, 11, 12, 13, 14)

        def norm(i, carry):
            rows = pl.ds(pl.multiple_of(i * 16, 16), 16)
            wide = xg[c, rows, :].astype(F32)
            mean_square = jnp.sum(wide * wide, axis=1, keepdims=True) * (1.0 / D)
            nb[rows, :] = (wide * lax.rsqrt(mean_square + EPSILON) * gains[0:1, :]).astype(BF16)
            return carry

        lax.fori_loop(0, ROWS // 16, norm, 0)

        def into(i, carry):
            cols = pl.ds(pl.multiple_of(i * TILE, TILE), TILE)
            gate = jnp.dot(nb[...], wg[:, cols], preferred_element_type=F32)
            up = jnp.dot(nb[...], wu[:, cols], preferred_element_type=F32)
            hb[:, cols] = (gate / (1.0 + jnp.exp(-gate)) * up).astype(BF16)
            return carry

        lax.fori_loop(0, H_DEV // TILE, into, 0)

        def out_of(i, carry):
            cols = pl.ds(pl.multiple_of(i * TILE, TILE), TILE)
            turned = jnp.dot(hb[...], wd[:, cols], preferred_element_type=F32)
            squares = jnp.dot((turned * turned).astype(BF16), ones[...], preferred_element_type=F32)
            limit = CLIP_FACTOR * jnp.sqrt(squares * (1.0 / 128.0) + BLOCK_EPSILON)
            rot[c, :, cols] = jnp.clip(turned, -limit, limit).astype(BF16)
            return carry

        lax.fori_loop(0, D // TILE, out_of, 0)
        start(c, 15, 16, 17, 18)

    def add(c, low, high, yy, zz, *others):
        total = rot[c, low:high, columns(yy, zz)].astype(F32)
        for other in others:
            total = total + other.astype(F32)
        rot[c, low:high, columns(yy, zz)] = total.astype(BF16)

    def sum_two(c):
        arrive(c, 15, 16)
        add(c, 0, LO, yf, z, land1[c, 0:LO])
        add(c, HI, ROWS, yf, z, land1[c, HI:ROWS])
        start(c, 19, 20)
        arrive(c, 17)
        add(c, LO, HALF, yp, zb, land1[c, LO:HALF])
        start(c, 21)
        arrive(c, 18)
        add(c, HALF, HI, ym, zb, land1[c, HALF:HI])
        start(c, 22, 23, 24, 25, 26)

    def sum_three(c):
        arrive(c, 19, 23, 24)
        add(c, 0, LO, yp, z, land2[c, 0:LO], land2[c, 544:592])
        add(c, LO, HALF, yp, z, land2[c, LO:HALF])
        add(c, HI, ROWS, yp, z, land2[c, 592:656])
        start(c, 27)
        arrive(c, 20, 25, 26)
        add(c, 0, LO, ym, z, land2[c, 656:704])
        add(c, HALF, HI, ym, z, land2[c, HALF:HI])
        add(c, HI, ROWS, ym, z, land2[c, HI:ROWS], land2[c, 704:768])
        start(c, 28)
        arrive(c, 21, 22)
        add(c, LO, HI, y, zb, land2[c, 256:400], land2[c, 400:544])
        start(c, 29)

    def finish(c):
        arrive(c, 27, 28, 29)
        out_rows = pl.ds(pl.multiple_of(c * ROWS, ROWS), ROWS)
        for j in range(PART // 128):
            cols = pl.ds(pl.multiple_of((y * 2 + z) * PART + j * 128, 128), 128)
            here = slice(j * 128, (j + 1) * 128)
            total = rot[c, :, cols].astype(F32)
            for i in range(3):
                total = total + land3[c, i, :, here].astype(F32)
            high = total.astype(BF16)
            low = (total - high.astype(F32)).astype(BF16)
            table = hada[0:128, 0:128]
            update = jnp.dot(high, table, preferred_element_type=F32)
            update = update + jnp.dot(low, table, preferred_element_type=F32)
            incoming = xg[c, :, cols].astype(F32)
            out_ref[out_rows, here] = (incoming + update * (1.0 / math.sqrt(128.0))).astype(BF16)

    def step(i, carry):
        def stage(lag, work):
            @pl.when(jnp.logical_and(i >= lag, i < lag + CHUNKS))
            def _():
                work(i - lag)

        stage(0, gather_one)
        stage(1, gather_two)
        stage(2, gather_three)

        @pl.when(i == 0)
        def _():
            loads[0].wait()

        @pl.when(i < 3)
        def _():
            turn_weights(i * 4, 4)

        @pl.when(i == 3)
        def _():
            loads[1].wait()
            loads[2].wait()
            for q in range(1, n_tp):
                gain_copy(q).wait_recv()

        stage(3, compute)
        stage(4, sum_two)
        stage(5, sum_three)
        stage(6, finish)
        return carry

    lax.fori_loop(0, CHUNKS + 6, step, 0)

    def drain(c, carry):
        for k in range(COPIES):
            copy(c, k).wait_send()

        @pl.when(has_next)
        def _():
            relay(c).wait_send()

        return carry

    lax.fori_loop(0, CHUNKS, drain, 0)
    for q in range(1, n_tp):
        gain_copy(q).wait_send()


def local(fresh_input, previous_out, norm_gain, gate_weight, up_weight, down_weight):
    anywhere = pl.BlockSpec(memory_space=pl.ANY)
    vmem = pl.BlockSpec(memory_space=pltpu.VMEM)
    dma = pltpu.SemaphoreType.DMA
    return pl.pallas_call(
        kernel,
        out_shape=jax.ShapeDtypeStruct((TOK, PART), BF16),
        in_specs=[anywhere, anywhere, vmem, anywhere, anywhere, anywhere],
        out_specs=vmem,
        scratch_shapes=[
            pltpu.VMEM((CHUNKS, ROWS, D), BF16),
            pltpu.VMEM((D, H_DEV), BF16),
            pltpu.VMEM((D, H_DEV), BF16),
            pltpu.VMEM((H_DEV, D), BF16),
            pltpu.VMEM((CHUNKS, ROWS, D), BF16),
            pltpu.VMEM((CHUNKS, ROWS, PART), BF16),
            pltpu.VMEM((CHUNKS, 3 * ROWS, PART), BF16),
            pltpu.VMEM((CHUNKS, 3, ROWS, PART), BF16),
            pltpu.VMEM((ROWS, D), BF16),
            pltpu.VMEM((ROWS, H_DEV), BF16),
            pltpu.VMEM((8, D), F32),
            pltpu.VMEM((TILE, TILE), BF16),
            pltpu.VMEM((TILE, TILE), BF16),
            dma((3,)),
            dma((CHUNKS,)),
            dma((CHUNKS,)),
            dma((CHUNKS,)),
            dma((7,)),
            dma((7,)),
            dma((CHUNKS, COPIES)),
            dma((CHUNKS, COPIES)),
        ],
        compiler_params=pltpu.CompilerParams(
            collective_id=0, has_side_effects=True, vmem_limit_bytes=56 << 20
        ),
        cost_estimate=pl.CostEstimate(
            flops=2 * 3 * TOK * D * H_DEV, bytes_accessed=3 * 2 * D * H_DEV, transcendentals=TOK * H_DEV
        ),
        name="relayed_feed_forward",
    )(fresh_input, previous_out, norm_gain, gate_weight, up_weight, down_weight)


def solution(mesh):
    in_specs = (
        P(None, "tp"),
        P("section", "tp"),
        P("section", "tp"),
        P("section", None, "tp"),
        P("section", None, "tp"),
        P("section", "tp", None),
    )
    return jax.shard_map(local, mesh=mesh, in_specs=in_specs, out_specs=P("section", "tp"), check_vma=False)
```

time: 493 us -> 114 us (0.23)
  waiting for transfers between devices: 388 us -> 0 us
  Pallas kernels: 0 us -> 112 us
  matrix products: 46.7 us -> 0 us
  blocking collectives: 24.9 us -> 0 us
  between operations: 13.5 us -> 0.01 us
  other arithmetic: 10.6 us -> 0 us
    psum x1 -> x0, waiting for transfers between devices: 269 us -> none  [local(): lax.psum(rotated.astype(jnp.bfloat16), 'tp').astype(jnp.float32)]
    all_gather x1 -> x0, waiting for transfers between devices: 117 us -> none  [local(): lax.all_gather(current, 'tp', axis=1, tiled=True)]
    pallas_call x0 -> x1, Pallas kernels: none -> 112 us  [local(): pl.pallas_call(kernel, out_shape=jax.ShapeDtypeStruct((TOK, PART), BF16),...]
    dot_general x5 -> x0, matrix products: 46.7 us -> none  [the longest x2 17.6 us: rotate(): jnp.einsum('...k,kj->...j', blocks, hadamard, precision=lax.Precision.HIG...]
    all_gather x1 -> x0, blocking collectives: 24.9 us -> none  [local(): lax.all_gather(norm_gain, 'tp', axis=1, tiled=True)]
  transfers between devices with their start and end apart: 3 -> 0, of which waited for: 3 -> 0; matrix products, arithmetic and copies ran while one was open for 0% -> 0% of each run, Pallas kernels for 0% -> 0%
where the time goes in v1:
time: 114 us
  Pallas kernels  112 us (98%)
  local copies, waits for them, and re-layouts  2.09 us (2%)
    pallas_call x1, Pallas kernels, local(): pl.pallas_call(kernel, out_shape=jax.ShapeDtypeStruct((TOK, PART), BF16),...  112 us

profile of v1, /device:TPU:0, one launch (start us, length us, event | category | flops | bytes accessed | tf_op | source)
XLA Modules:
  0.0 113.9 jit_solution(6514561325831613249)
XLA Ops:
  0.0 111.8 %relayed_feed_forward.1 = bf16[1024,384]{1,0:T(8,128)(2,1)} custom-call(bf16[1024,384]{1,0:T(8,128)(2,1)} %fresh_ref.1, bf16[1024,384]{1,0:T(8,128)(2,1)} %prev_ref.1, bf16[1,384]{1,0:T(2,128)(2,1)} %gain_ref.1, bf16[1,3072,1024]{2,1,0:T(8,128)(2,1)} %gate_ref.1, bf16[1,3072,1024]{2,1,0:T(8,128)(2,1)} %up_ref.1, bf16[1,1024,3072]{2,1,0:T(8,128)(2,1)} %down_ref.1), custom_call_target="tpu_custom_call" | custom-call | flops 19327352832 | bytes 18874368 | tf_op jit(solution)/shard_map/relayed_feed_forward/pallas_call | solution.py:361
  111.8 2.1 %copy.8 = bf16[1024,384]{1,0:T(8,128)(2,1)} copy(bf16[1024,384]{1,0:T(8,128)(2,1)} %relayed_feed_forward.1) | data formatting | bytes 1572864

commit v2 on v1

--- a/solution.py
+++ b/solution.py
@@ -23,8 +23,13 @@
 CHUNKS = TOK // ROWS
 TILE = 256
 COPIES = 30
+NORM_ROWS = 64
 
 LO, HALF, HI = 48, 128, 192
+S_LO, S_HI = 48, 192
+MIDDLE = S_HI - S_LO
+EDGE = ROWS - MIDDLE
+EDGES = ROWS + 2 * MIDDLE
 
 
 def kernel(
@@ -152,18 +157,18 @@
 
     def summed(c, k):
         low, high, yy, zz, dev, dst = (
-            (0, LO, yf, zb, dev_z, land1.at[c, pl.ds(0, LO)]),
-            (HI, ROWS, yf, zb, dev_z, land1.at[c, pl.ds(HI, ROWS - HI)]),
-            (LO, HALF, yf, zb, dev_p, land1.at[c, pl.ds(LO, HALF - LO)]),
-            (HALF, HI, yf, zb, dev_m, land1.at[c, pl.ds(HALF, HI - HALF)]),
+            (0, S_LO, yf, zb, dev_z, land1.at[c, pl.ds(0, S_LO)]),
+            (S_HI, ROWS, yf, zb, dev_z, land1.at[c, pl.ds(S_HI, ROWS - S_HI)]),
+            (S_LO, HALF, yf, zb, dev_p, land1.at[c, pl.ds(S_LO, HALF - S_LO)]),
+            (HALF, S_HI, yf, zb, dev_m, land1.at[c, pl.ds(HALF, S_HI - HALF)]),
             (0, HALF, yf, z, dev_p, land2.at[c, pl.ds(0, HALF)]),
             (HALF, ROWS, yf, z, dev_m, land2.at[c, pl.ds(HALF, ROWS - HALF)]),
-            (LO, HI, yp, zb, dev_p, land2.at[c, pl.ds(256, HI - LO)]),
-            (LO, HI, ym, zb, dev_m, land2.at[c, pl.ds(400, HI - LO)]),
-            (0, LO, yp, zb, dev_z, land2.at[c, pl.ds(544, LO)]),
-            (HI, ROWS, yp, zb, dev_z, land2.at[c, pl.ds(592, ROWS - HI)]),
-            (0, LO, ym, zb, dev_z, land2.at[c, pl.ds(656, LO)]),
-            (HI, ROWS, ym, zb, dev_z, land2.at[c, pl.ds(704, ROWS - HI)]),
+            (S_LO, S_HI, yp, zb, dev_p, land2.at[c, pl.ds(ROWS, MIDDLE)]),
+            (S_LO, S_HI, ym, zb, dev_m, land2.at[c, pl.ds(ROWS + MIDDLE, MIDDLE)]),
+            (0, S_LO, yp, zb, dev_z, land2.at[c, pl.ds(EDGES, S_LO)]),
+            (S_HI, ROWS, yp, zb, dev_z, land2.at[c, pl.ds(EDGES + S_LO, ROWS - S_HI)]),
+            (0, S_LO, ym, zb, dev_z, land2.at[c, pl.ds(EDGES + EDGE, S_LO)]),
+            (S_HI, ROWS, ym, zb, dev_z, land2.at[c, pl.ds(EDGES + EDGE + S_LO, ROWS - S_HI)]),
             (0, ROWS, yp, z, dev_p, land3.at[c, 0]),
             (0, ROWS, ym, z, dev_m, land3.at[c, 1]),
             (0, ROWS, y, zb, dev_z, land3.at[c, 2]),
@@ -228,32 +233,23 @@
         arrive(c, 7, 8, 9, 10, 11, 12, 13, 14)
 
         def norm(i, carry):
-            rows = pl.ds(pl.multiple_of(i * 16, 16), 16)
+            rows = pl.ds(pl.multiple_of(i * NORM_ROWS, NORM_ROWS), NORM_ROWS)
             wide = xg[c, rows, :].astype(F32)
             mean_square = jnp.sum(wide * wide, axis=1, keepdims=True) * (1.0 / D)
             nb[rows, :] = (wide * lax.rsqrt(mean_square + EPSILON) * gains[0:1, :]).astype(BF16)
             return carry
 
-        lax.fori_loop(0, ROWS // 16, norm, 0)
-
-        def into(i, carry):
-            cols = pl.ds(pl.multiple_of(i * TILE, TILE), TILE)
-            gate = jnp.dot(nb[...], wg[:, cols], preferred_element_type=F32)
-            up = jnp.dot(nb[...], wu[:, cols], preferred_element_type=F32)
-            hb[:, cols] = (gate / (1.0 + jnp.exp(-gate)) * up).astype(BF16)
-            return carry
-
-        lax.fori_loop(0, H_DEV // TILE, into, 0)
-
-        def out_of(i, carry):
-            cols = pl.ds(pl.multiple_of(i * TILE, TILE), TILE)
-            turned = jnp.dot(hb[...], wd[:, cols], preferred_element_type=F32)
+        lax.fori_loop(0, ROWS // NORM_ROWS, norm, 0)
+        gate = jnp.dot(nb[...], wg[...], preferred_element_type=F32)
+        up = jnp.dot(nb[...], wu[...], preferred_element_type=F32)
+        hb[...] = (gate / (1.0 + jnp.exp(-gate)) * up).astype(BF16)
+        term = jnp.dot(hb[...], wd[...], preferred_element_type=F32)
+        for j in range(0, D, TILE):
+            turned = term[:, j : j + TILE]
             squares = jnp.dot((turned * turned).astype(BF16), ones[...], preferred_element_type=F32)
-            limit = CLIP_FACTOR * jnp.sqrt(squares * (1.0 / 128.0) + BLOCK_EPSILON)
-            rot[c, :, cols] = jnp.clip(turned, -limit, limit).astype(BF16)
-            return carry
-
-        lax.fori_loop(0, D // TILE, out_of, 0)
+            fourfold = squares * (CLIP_FACTOR**2 / 128.0) + CLIP_FACTOR**2 * BLOCK_EPSILON
+            limit = fourfold * lax.rsqrt(fourfold)
+            rot[c, :, j : j + TILE] = jnp.minimum(jnp.maximum(turned, -limit), limit).astype(BF16)
         start(c, 15, 16, 17, 18)
 
     def add(c, low, high, yy, zz, *others):
@@ -264,29 +260,29 @@
 
     def sum_two(c):
         arrive(c, 15, 16)
-        add(c, 0, LO, yf, z, land1[c, 0:LO])
-        add(c, HI, ROWS, yf, z, land1[c, HI:ROWS])
+        add(c, 0, S_LO, yf, z, land1[c, 0:S_LO])
+        add(c, S_HI, ROWS, yf, z, land1[c, S_HI:ROWS])
         start(c, 19, 20)
         arrive(c, 17)
-        add(c, LO, HALF, yp, zb, land1[c, LO:HALF])
+        add(c, S_LO, HALF, yp, zb, land1[c, S_LO:HALF])
         start(c, 21)
         arrive(c, 18)
-        add(c, HALF, HI, ym, zb, land1[c, HALF:HI])
+        add(c, HALF, S_HI, ym, zb, land1[c, HALF:S_HI])
         start(c, 22, 23, 24, 25, 26)
 
     def sum_three(c):
         arrive(c, 19, 23, 24)
-        add(c, 0, LO, yp, z, land2[c, 0:LO], land2[c, 544:592])
-        add(c, LO, HALF, yp, z, land2[c, LO:HALF])
-        add(c, HI, ROWS, yp, z, land2[c, 592:656])
+        add(c, 0, S_LO, yp, z, land2[c, 0:S_LO], land2[c, EDGES : EDGES + S_LO])
+        add(c, S_LO, HALF, yp, z, land2[c, S_LO:HALF])
+        add(c, S_HI, ROWS, yp, z, land2[c, EDGES + S_LO : EDGES + EDGE])
         start(c, 27)
         arrive(c, 20, 25, 26)
-        add(c, 0, LO, ym, z, land2[c, 656:704])
-        add(c, HALF, HI, ym, z, land2[c, HALF:HI])
-        add(c, HI, ROWS, ym, z, land2[c, HI:ROWS], land2[c, 704:768])
+        add(c, 0, S_LO, ym, z, land2[c, EDGES + EDGE : EDGES + EDGE + S_LO])
+        add(c, HALF, S_HI, ym, z, land2[c, HALF:S_HI])
+        add(c, S_HI, ROWS, ym, z, land2[c, S_HI:ROWS], land2[c, EDGES + EDGE + S_LO : EDGES + 2 * EDGE])
         start(c, 28)
         arrive(c, 21, 22)
-        add(c, LO, HI, y, zb, land2[c, 256:400], land2[c, 400:544])
+        add(c, S_LO, S_HI, y, zb, land2[c, ROWS : ROWS + MIDDLE], land2[c, ROWS + MIDDLE : EDGES])
         start(c, 29)
 
     def finish(c):

time: 114 us -> 97.9 us (0.86); the launches traced: 114 us -> 96.5 us
  Pallas kernels: 112 us -> 94.4 us
    pallas_call x1, Pallas kernels: 112 us -> 94.4 us  [local(): pl.pallas_call(kernel, out_shape=jax.ShapeDtypeStruct((TOK, PART), BF16),...]
where the time goes in v2:
time: 97.9 us; the launch traced here: 96.5 us
  Pallas kernels  94.4 us (96%)
  local copies, waits for them, and re-layouts  2.09 us (2%)
    pallas_call x1, Pallas kernels, local(): pl.pallas_call(kernel, out_shape=jax.ShapeDtypeStruct((TOK, PART), BF16),...  94.4 us
    unnamed x1, local copies, waits for them, and re-layouts  2.09 us

profile of v2, /device:TPU:0, one launch (start us, length us, event | category | flops | bytes accessed | tf_op | source)
XLA Modules:
  0.0 96.5 jit_solution(11272591045318508373)
XLA Ops:
  0.0 94.4 %relayed_feed_forward.1 = bf16[1024,384]{1,0:T(8,128)(2,1)} custom-call(bf16[1024,384]{1,0:T(8,128)(2,1)} %fresh_ref.1, bf16[1024,384]{1,0:T(8,128)(2,1)} %prev_ref.1, bf16[1,384]{1,0:T(2,128)(2,1)} %gain_ref.1, bf16[1,3072,1024]{2,1,0:T(8,128)(2,1)} %gate_ref.1, bf16[1,3072,1024]{2,1,0:T(8,128)(2,1)} %up_ref.1, bf16[1,1024,3072]{2,1,0:T(8,128)(2,1)} %down_ref.1), custom_call_target="tpu_custom_call" | custom-call | flops 19327352832 | bytes 18874368 | tf_op jit(solution)/shard_map/relayed_feed_forward/pallas_call | solution.py:357
  94.4 2.1 %copy.8 = bf16[1024,384]{1,0:T(8,128)(2,1)} copy(bf16[1024,384]{1,0:T(8,128)(2,1)} %relayed_feed_forward.1) | data formatting | bytes 1572864

commit v3 on v2

--- a/solution.py
+++ b/solution.py
@@ -23,10 +23,13 @@
 CHUNKS = TOK // ROWS
 TILE = 256
 COPIES = 30
+PIECES = 4
+PIECE = ROWS // PIECES
+SLOTS = PIECES - 1 + CHUNKS
 NORM_ROWS = 64
 
 LO, HALF, HI = 48, 128, 192
-S_LO, S_HI = 48, 192
+S_LO, S_HALF, S_HI = 64, 128, 208
 MIDDLE = S_HI - S_LO
 EDGE = ROWS - MIDDLE
 EDGES = ROWS + 2 * MIDDLE
@@ -34,8 +37,8 @@
 
 def kernel(
     fresh_ref, prev_ref, gain_ref, gate_ref, up_ref, down_ref, out_ref,
-    xg, wg, wu, wd, rot, land1, land2, land3, nb, hb, gains, hada, ones,
-    load_sem, fresh_sem, relay_send, relay_recv, gain_send, gain_recv, send, recv,
+    xg, wg, wu, wd, rot, done, land1, land2, land3, nb, hb, gains, hada, ones,
+    out_sem, load_sem, fresh_sem, relay_send, relay_recv, first_send, first_recv, gain_send, gain_recv, send, recv,
 ):
     s = lax.axis_index("section")
     t = lax.axis_index("tp")
@@ -77,44 +80,63 @@
     def columns(yy, zz):
         return pl.ds(pl.multiple_of((yy * 2 + zz) * PART, 128), PART)
 
-    def relay(c):
+    def source(ref, slot):
+        if isinstance(slot, int) and slot < PIECES:
+            return ref.at[pl.ds(slot * PIECE, PIECE)], xg.at[0, pl.ds(slot * PIECE, PIECE), columns(y, z)]
+        c = slot - (PIECES - 1)
+        return ref.at[pl.ds(pl.multiple_of(c * ROWS, ROWS), ROWS)], xg.at[c, :, columns(y, z)]
+
+    def relay(slot):
+        src, dst = source(prev_ref, slot)
         return pltpu.make_async_remote_copy(
-            prev_ref.at[pl.ds(pl.multiple_of(c * ROWS, ROWS), ROWS)],
-            xg.at[c, :, columns(y, z)],
-            relay_send.at[c],
-            relay_recv.at[c],
-            device_id=next_dev,
-            device_id_type=MESH,
+            src, dst, relay_send.at[slot], relay_recv.at[slot], device_id=next_dev, device_id_type=MESH
         )
 
-    def fresh(c):
-        return pltpu.make_async_copy(
-            fresh_ref.at[pl.ds(pl.multiple_of(c * ROWS, ROWS), ROWS)],
-            xg.at[c, :, columns(y, z)],
-            fresh_sem.at[c],
-        )
+    def fresh(slot):
+        src, dst = source(fresh_ref, slot)
+        return pltpu.make_async_copy(src, dst, fresh_sem.at[slot])
 
     @pl.when(has_next)
     def _():
-        for c in range(CHUNKS):
-            relay(c).start()
+        for slot in range(SLOTS):
+            relay(slot).start()
 
     @pl.when(s == 0)
     def _():
-        for c in range(CHUNKS):
-            fresh(c).start()
+        for slot in range(SLOTS):
+            fresh(slot).start()
+
+    def incoming_rows(slot):
+        @pl.when(s == 0)
+        def _():
+            fresh(slot).wait()
+
+        @pl.when(has_prev)
+        def _():
+            relay(slot).wait_recv()
+
+    def first(p, d):
+        ref = xg.at[0, pl.ds(p * PIECE, PIECE), columns(y, zo)]
+        return pltpu.make_async_remote_copy(
+            ref, ref, first_send.at[p, d], first_recv.at[p, d], device_id=(dev_z, dev_p, dev_m)[d], device_id_type=MESH
+        )
+
+    for p in range(PIECES):
+        incoming_rows(p)
+        for d in range(3):
+            first(p, d).start()
 
     def gain_copy(q):
         return pltpu.make_async_remote_copy(
-            gains.at[:, columns(y, z)],
-            gains.at[:, columns(y, z)],
+            gains.at[pl.ds(0, 1), columns(y, z)],
+            gains.at[pl.ds(0, 1), columns(y, z)],
             gain_send.at[q - 1],
             gain_recv.at[q - 1],
             device_id=(s, (t + q) % n_tp),
             device_id_type=MESH,
         )
 
-    gains[:, columns(y, z)] = jnp.broadcast_to(gain_ref[...].astype(F32), (8, PART))
+    gains[0:1, columns(y, z)] = gain_ref[...].astype(F32)
     for q in range(1, n_tp):
         gain_copy(q).start()
 
@@ -159,10 +181,10 @@
         low, high, yy, zz, dev, dst = (
             (0, S_LO, yf, zb, dev_z, land1.at[c, pl.ds(0, S_LO)]),
             (S_HI, ROWS, yf, zb, dev_z, land1.at[c, pl.ds(S_HI, ROWS - S_HI)]),
-            (S_LO, HALF, yf, zb, dev_p, land1.at[c, pl.ds(S_LO, HALF - S_LO)]),
-            (HALF, S_HI, yf, zb, dev_m, land1.at[c, pl.ds(HALF, S_HI - HALF)]),
-            (0, HALF, yf, z, dev_p, land2.at[c, pl.ds(0, HALF)]),
-            (HALF, ROWS, yf, z, dev_m, land2.at[c, pl.ds(HALF, ROWS - HALF)]),
+            (S_LO, S_HALF, yf, zb, dev_p, land1.at[c, pl.ds(S_LO, S_HALF - S_LO)]),
+            (S_HALF, S_HI, yf, zb, dev_m, land1.at[c, pl.ds(S_HALF, S_HI - S_HALF)]),
+            (0, S_HALF, yf, z, dev_p, land2.at[c, pl.ds(0, S_HALF)]),
+            (S_HALF, ROWS, yf, z, dev_m, land2.at[c, pl.ds(S_HALF, ROWS - S_HALF)]),
             (S_LO, S_HI, yp, zb, dev_p, land2.at[c, pl.ds(ROWS, MIDDLE)]),
             (S_LO, S_HI, ym, zb, dev_m, land2.at[c, pl.ds(ROWS + MIDDLE, MIDDLE)]),
             (0, S_LO, yp, zb, dev_z, land2.at[c, pl.ds(EDGES, S_LO)]),
@@ -190,22 +212,27 @@
             copy(c, k).wait_recv()
 
     def gather_one(c):
-        @pl.when(s == 0)
-        def _():
-            fresh(c).wait()
-
-        @pl.when(has_prev)
-        def _():
-            relay(c).wait_recv()
-
-        start(c, 0, 1, 2)
+        @pl.when(c > 0)
+        def _():
+            incoming_rows(PIECES - 1 + c)
+            start(c, 0, 1, 2)
+
+    def arrive_own(c, d):
+        @pl.when(c == 0)
+        def _():
+            for p in range(PIECES):
+                first(p, d).wait_recv()
+
+        @pl.when(c > 0)
+        def _():
+            arrive(c, d)
 
     def gather_two(c):
-        arrive(c, 1)
+        arrive_own(c, 1)
         start(c, 5, 7, 8)
-        arrive(c, 2)
+        arrive_own(c, 2)
         start(c, 6, 9, 10)
-        arrive(c, 0)
+        arrive_own(c, 0)
         start(c, 3, 4)
 
     def gather_three(c):
@@ -220,14 +247,12 @@
 
     def turn_weights(first, count):
         def body(i, carry):
-            at = first * 4 + i
-            rows = pl.ds(pl.multiple_of((at % 4) * 256, 256), 256)
-            cols = pl.ds(pl.multiple_of((at // 4) * TILE, TILE), TILE)
-            turned = jnp.dot(wd[rows, cols], hada[...], preferred_element_type=F32)
-            wd[rows, cols] = (turned * (1.0 / math.sqrt(128.0))).astype(BF16)
+            cols = pl.ds(pl.multiple_of((first + i) * TILE, TILE), TILE)
+            turned = jnp.dot(wd[:, cols], hada[...], preferred_element_type=F32)
+            wd[:, cols] = (turned * (1.0 / math.sqrt(128.0))).astype(BF16)
             return carry
 
-        lax.fori_loop(0, count * 4, body, 0)
+        lax.fori_loop(0, count, body, 0)
 
     def compute(c):
         arrive(c, 7, 8, 9, 10, 11, 12, 13, 14)
@@ -243,6 +268,7 @@
         gate = jnp.dot(nb[...], wg[...], preferred_element_type=F32)
         up = jnp.dot(nb[...], wu[...], preferred_element_type=F32)
         hb[...] = (gate / (1.0 + jnp.exp(-gate)) * up).astype(BF16)
+    def compute_out(c):
         term = jnp.dot(hb[...], wd[...], preferred_element_type=F32)
         for j in range(0, D, TILE):
             turned = term[:, j : j + TILE]
@@ -264,21 +290,21 @@
         add(c, S_HI, ROWS, yf, z, land1[c, S_HI:ROWS])
         start(c, 19, 20)
         arrive(c, 17)
-        add(c, S_LO, HALF, yp, zb, land1[c, S_LO:HALF])
+        add(c, S_LO, S_HALF, yp, zb, land1[c, S_LO:S_HALF])
         start(c, 21)
         arrive(c, 18)
-        add(c, HALF, S_HI, ym, zb, land1[c, HALF:S_HI])
+        add(c, S_HALF, S_HI, ym, zb, land1[c, S_HALF:S_HI])
         start(c, 22, 23, 24, 25, 26)
 
     def sum_three(c):
         arrive(c, 19, 23, 24)
         add(c, 0, S_LO, yp, z, land2[c, 0:S_LO], land2[c, EDGES : EDGES + S_LO])
-        add(c, S_LO, HALF, yp, z, land2[c, S_LO:HALF])
+        add(c, S_LO, S_HALF, yp, z, land2[c, S_LO:S_HALF])
         add(c, S_HI, ROWS, yp, z, land2[c, EDGES + S_LO : EDGES + EDGE])
         start(c, 27)
         arrive(c, 20, 25, 26)
         add(c, 0, S_LO, ym, z, land2[c, EDGES + EDGE : EDGES + EDGE + S_LO])
-        add(c, HALF, S_HI, ym, z, land2[c, HALF:S_HI])
+        add(c, S_HALF, S_HI, ym, z, land2[c, S_HALF:S_HI])
         add(c, S_HI, ROWS, ym, z, land2[c, S_HI:ROWS], land2[c, EDGES + EDGE + S_LO : EDGES + 2 * EDGE])
         start(c, 28)
         arrive(c, 21, 22)
@@ -300,7 +326,13 @@
             update = jnp.dot(high, table, preferred_element_type=F32)
             update = update + jnp.dot(low, table, preferred_element_type=F32)
             incoming = xg[c, :, cols].astype(F32)
-            out_ref[out_rows, here] = (incoming + update * (1.0 / math.sqrt(128.0))).astype(BF16)
+            done[out_rows, here] = (incoming + update * (1.0 / math.sqrt(128.0))).astype(BF16)
+
+        written(c).start()
+
+    def written(c):
+        rows = pl.ds(pl.multiple_of(c * ROWS, ROWS), ROWS)
+        return pltpu.make_async_copy(done.at[rows], out_ref.at[rows], out_sem.at[c])
 
     def step(i, carry):
         def stage(lag, work):
@@ -329,6 +361,7 @@
 
         stage(3, compute)
         stage(4, sum_two)
+        stage(3, compute_out)
         stage(5, sum_three)
         stage(6, finish)
         return carry
@@ -336,16 +369,28 @@
     lax.fori_loop(0, CHUNKS + 6, step, 0)
 
     def drain(c, carry):
-        for k in range(COPIES):
+        @pl.when(c > 0)
+        def _():
+            for k in range(3):
+                copy(c, k).wait_send()
+
+        for k in range(3, COPIES):
             copy(c, k).wait_send()
 
-        @pl.when(has_next)
-        def _():
-            relay(c).wait_send()
+        written(c).wait()
 
         return carry
 
     lax.fori_loop(0, CHUNKS, drain, 0)
+    for p in range(PIECES):
+        for d in range(3):
+            first(p, d).wait_send()
+
+    @pl.when(has_next)
+    def _():
+        for slot in range(SLOTS):
+            relay(slot).wait_send()
+
     for q in range(1, n_tp):
         gain_copy(q).wait_send()
 
@@ -358,13 +403,14 @@
         kernel,
         out_shape=jax.ShapeDtypeStruct((TOK, PART), BF16),
         in_specs=[anywhere, anywhere, vmem, anywhere, anywhere, anywhere],
-        out_specs=vmem,
+        out_specs=anywhere,
         scratch_shapes=[
             pltpu.VMEM((CHUNKS, ROWS, D), BF16),
             pltpu.VMEM((D, H_DEV), BF16),
             pltpu.VMEM((D, H_DEV), BF16),
             pltpu.VMEM((H_DEV, D), BF16),
             pltpu.VMEM((CHUNKS, ROWS, D), BF16),
+            pltpu.VMEM((TOK, PART), BF16),
             pltpu.VMEM((CHUNKS, ROWS, PART), BF16),
             pltpu.VMEM((CHUNKS, 3 * ROWS, PART), BF16),
             pltpu.VMEM((CHUNKS, 3, ROWS, PART), BF16),
@@ -373,10 +419,13 @@
             pltpu.VMEM((8, D), F32),
             pltpu.VMEM((TILE, TILE), BF16),
             pltpu.VMEM((TILE, TILE), BF16),
+            dma((CHUNKS,)),
             dma((3,)),
-            dma((CHUNKS,)),
-            dma((CHUNKS,)),
-            dma((CHUNKS,)),
+            dma((SLOTS,)),
+            dma((SLOTS,)),
+            dma((SLOTS,)),
+            dma((PIECES, 3)),
+            dma((PIECES, 3)),
             dma((7,)),
             dma((7,)),
             dma((CHUNKS, COPIES)),

time: 97.9 us -> 94.9 us (0.969)
  Pallas kernels: 94.4 us -> 91.7 us
    pallas_call x1, Pallas kernels: 94.4 us -> 91.7 us  [local(): pl.pallas_call(kernel, out_shape=jax.ShapeDtypeStruct((TOK, PART), BF16),...]
where the time goes in v3:
time: 94.9 us; the launch traced here: 93.8 us
  Pallas kernels  91.7 us (97%)
  local copies, waits for them, and re-layouts  2.09 us (2%)
    pallas_call x1, Pallas kernels, local(): pl.pallas_call(kernel, out_shape=jax.ShapeDtypeStruct((TOK, PART), BF16),...  91.7 us
    unnamed x1, local copies, waits for them, and re-layouts  2.09 us

profile of v3, /device:TPU:0, one launch (start us, length us, event | category | flops | bytes accessed | tf_op | source)
XLA Modules:
  0.0 93.8 jit_solution(16243153396989751459)
XLA Ops:
  0.0 91.7 %relayed_feed_forward.1 = bf16[1024,384]{1,0:T(8,128)(2,1)} custom-call(bf16[1024,384]{1,0:T(8,128)(2,1)} %fresh_ref.1, bf16[1024,384]{1,0:T(8,128)(2,1)} %prev_ref.1, bf16[1,384]{1,0:T(2,128)(2,1)} %gain_ref.1, bf16[1,3072,1024]{2,1,0:T(8,128)(2,1)} %gate_ref.1, bf16[1,3072,1024]{2,1,0:T(8,128)(2,1)} %up_ref.1, bf16[1,1024,3072]{2,1,0:T(8,128)(2,1)} %down_ref.1), custom_call_target="tpu_custom_call" | custom-call | flops 19327352832 | bytes 18874368 | tf_op jit(solution)/shard_map/relayed_feed_forward/pallas_call | solution.py:402
  91.7 2.1 %copy.8 = bf16[1024,384]{1,0:T(8,128)(2,1)} copy(bf16[1024,384]{1,0:T(8,128)(2,1)} %relayed_feed_forward.1) | data formatting | bytes 1572864

commit v4 on v2

--- a/solution.py
+++ b/solution.py
@@ -18,24 +18,34 @@
 TOK = 1024
 D = 3072
 H_DEV = 1024
+N_TP = 8
 PART = 384
 ROWS = 256
 CHUNKS = TOK // ROWS
 TILE = 256
-COPIES = 30
 NORM_ROWS = 64
 
 LO, HALF, HI = 48, 128, 192
-S_LO, S_HI = 48, 192
+S_LO, S_HALF, S_HI = 64, 128, 208
 MIDDLE = S_HI - S_LO
 EDGE = ROWS - MIDDLE
 EDGES = ROWS + 2 * MIDDLE
 
+GROUPS = (
+    (0,), (1,), (2,), (3, 4), (5, 6), (7, 8, 9, 10, 11, 12, 13, 14),
+    (15, 16), (17, 18), (19, 23, 24), (20, 25, 26), (21, 22), (27, 28, 29),
+)
+GROUP_OF = {k: group for group, ks in enumerate(GROUPS) for k in ks}
+GROUP_ROWS = (
+    ROWS, ROWS, ROWS, 2 * (HI - LO), ROWS, 3 * (ROWS - HI + LO) + HI - LO,
+    EDGE, MIDDLE, S_HALF + EDGE, ROWS - S_HALF + EDGE, 2 * MIDDLE, 3 * ROWS,
+)
+
 
 def kernel(
     fresh_ref, prev_ref, gain_ref, gate_ref, up_ref, down_ref, out_ref,
-    xg, wg, wu, wd, rot, land1, land2, land3, nb, hb, gains, hada, ones,
-    load_sem, fresh_sem, relay_send, relay_recv, gain_send, gain_recv, send, recv,
+    xg, wg, wu, wd, rot, land1, land2, land3, nb, hb, gains, hada, ones, gain,
+    gain_sem, load_sem, relayed, gained, sent, landed,
 ):
     s = lax.axis_index("section")
     t = lax.axis_index("tp")
@@ -57,6 +67,8 @@
         pltpu.make_async_copy(src, dst, load_sem.at[i])
         for i, (src, dst) in enumerate(((down_ref.at[0], wd), (gate_ref.at[0], wg), (up_ref.at[0], wu)))
     ]
+    gain_load = pltpu.make_async_copy(gain_ref, gain, gain_sem)
+    gain_load.start()
     for load in loads:
         load.start()
 
@@ -77,21 +89,17 @@
     def columns(yy, zz):
         return pl.ds(pl.multiple_of((yy * 2 + zz) * PART, 128), PART)
 
+    def chunk_rows(c):
+        return pl.ds(pl.multiple_of(c * ROWS, ROWS), ROWS)
+
     def relay(c):
         return pltpu.make_async_remote_copy(
-            prev_ref.at[pl.ds(pl.multiple_of(c * ROWS, ROWS), ROWS)],
+            prev_ref.at[chunk_rows(c)],
             xg.at[c, :, columns(y, z)],
-            relay_send.at[c],
-            relay_recv.at[c],
+            sent.at[2],
+            relayed.at[c],
             device_id=next_dev,
             device_id_type=MESH,
-        )
-
-    def fresh(c):
-        return pltpu.make_async_copy(
-            fresh_ref.at[pl.ds(pl.multiple_of(c * ROWS, ROWS), ROWS)],
-            xg.at[c, :, columns(y, z)],
-            fresh_sem.at[c],
         )
 
     @pl.when(has_next)
@@ -102,21 +110,22 @@
     @pl.when(s == 0)
     def _():
         for c in range(CHUNKS):
-            fresh(c).start()
-
-    def gain_copy(q):
+            pltpu.make_async_copy(
+                fresh_ref.at[chunk_rows(c)], xg.at[c, :, columns(y, z)], relayed.at[c]
+            ).start()
+
+    def gain_copy(cols, dev):
+        row = gains.at[pl.ds(0, 1), cols]
         return pltpu.make_async_remote_copy(
-            gains.at[:, columns(y, z)],
-            gains.at[:, columns(y, z)],
-            gain_send.at[q - 1],
-            gain_recv.at[q - 1],
-            device_id=(s, (t + q) % n_tp),
-            device_id_type=MESH,
+            row, row, sent.at[3], gained, device_id=dev, device_id_type=MESH
         )
 
-    gains[:, columns(y, z)] = jnp.broadcast_to(gain_ref[...].astype(F32), (8, PART))
+    all_gains = gain_copy(pl.ds(0, (N_TP - 1) * PART), dev_z)
+
+    gain_load.wait()
+    gains[0:1, columns(y, z)] = gain[...].astype(F32)
     for q in range(1, n_tp):
-        gain_copy(q).start()
+        gain_copy(columns(y, z), (s, (t + q) % n_tp)).start()
 
     row_id = lax.broadcasted_iota(jnp.int32, (TILE, TILE), 0)
     col_id = lax.broadcasted_iota(jnp.int32, (TILE, TILE), 1)
@@ -159,10 +168,10 @@
         low, high, yy, zz, dev, dst = (
             (0, S_LO, yf, zb, dev_z, land1.at[c, pl.ds(0, S_LO)]),
             (S_HI, ROWS, yf, zb, dev_z, land1.at[c, pl.ds(S_HI, ROWS - S_HI)]),
-            (S_LO, HALF, yf, zb, dev_p, land1.at[c, pl.ds(S_LO, HALF - S_LO)]),
-            (HALF, S_HI, yf, zb, dev_m, land1.at[c, pl.ds(HALF, S_HI - HALF)]),
-            (0, HALF, yf, z, dev_p, land2.at[c, pl.ds(0, HALF)]),
-            (HALF, ROWS, yf, z, dev_m, land2.at[c, pl.ds(HALF, ROWS - HALF)]),
+            (S_LO, S_HALF, yf, zb, dev_p, land1.at[c, pl.ds(S_LO, S_HALF - S_LO)]),
+            (S_HALF, S_HI, yf, zb, dev_m, land1.at[c, pl.ds(S_HALF, S_HI - S_HALF)]),
+            (0, S_HALF, yf, z, dev_p, land2.at[c, pl.ds(0, S_HALF)]),
+            (S_HALF, ROWS, yf, z, dev_m, land2.at[c, pl.ds(S_HALF, ROWS - S_HALF)]),
             (S_LO, S_HI, yp, zb, dev_p, land2.at[c, pl.ds(ROWS, MIDDLE)]),
             (S_LO, S_HI, ym, zb, dev_m, land2.at[c, pl.ds(ROWS + MIDDLE, MIDDLE)]),
             (0, S_LO, yp, zb, dev_z, land2.at[c, pl.ds(EDGES, S_LO)]),
@@ -178,26 +187,21 @@
     def copy(c, k):
         src, dst, dev = gathered(c, k) if k < 15 else summed(c, k)
         return pltpu.make_async_remote_copy(
-            src, dst, send.at[c, k], recv.at[c, k], device_id=dev, device_id_type=MESH
+            src, dst, sent.at[k // 15], landed.at[c, GROUP_OF[k]], device_id=dev, device_id_type=MESH
         )
 
     def start(c, *ks):
         for k in ks:
             copy(c, k).start()
 
-    def arrive(c, *ks):
-        for k in ks:
-            copy(c, k).wait_recv()
+    def arrive(c, group):
+        rows = land2.at[c, pl.ds(0, GROUP_ROWS[group])]
+        pltpu.make_async_remote_copy(
+            rows, rows, sent.at[0], landed.at[c, group], device_id=dev_z, device_id_type=MESH
+        ).wait_recv()
 
     def gather_one(c):
-        @pl.when(s == 0)
-        def _():
-            fresh(c).wait()
-
-        @pl.when(has_prev)
-        def _():
-            relay(c).wait_recv()
-
+        relay(c).wait_recv()
         start(c, 0, 1, 2)
 
     def gather_two(c):
@@ -209,28 +213,22 @@
         start(c, 3, 4)
 
     def gather_three(c):
-        arrive(c, 5)
-        start(c, 11)
-        arrive(c, 6)
-        start(c, 12)
+        arrive(c, 4)
+        start(c, 11, 12)
         arrive(c, 3)
-        start(c, 13)
-        arrive(c, 4)
-        start(c, 14)
+        start(c, 13, 14)
 
     def turn_weights(first, count):
         def body(i, carry):
-            at = first * 4 + i
-            rows = pl.ds(pl.multiple_of((at % 4) * 256, 256), 256)
-            cols = pl.ds(pl.multiple_of((at // 4) * TILE, TILE), TILE)
-            turned = jnp.dot(wd[rows, cols], hada[...], preferred_element_type=F32)
-            wd[rows, cols] = (turned * (1.0 / math.sqrt(128.0))).astype(BF16)
+            cols = pl.ds(pl.multiple_of((first + i) * TILE, TILE), TILE)
+            turned = jnp.dot(wd[:, cols], hada[...], preferred_element_type=F32)
+            wd[:, cols] = (turned * (1.0 / math.sqrt(128.0))).astype(BF16)
             return carry
 
-        lax.fori_loop(0, count * 4, body, 0)
+        lax.fori_loop(0, count, body, 0)
 
     def compute(c):
-        arrive(c, 7, 8, 9, 10, 11, 12, 13, 14)
+        arrive(c, 5)
 
         def norm(i, carry):
             rows = pl.ds(pl.multiple_of(i * NORM_ROWS, NORM_ROWS), NORM_ROWS)
@@ -243,6 +241,7 @@
         gate = jnp.dot(nb[...], wg[...], preferred_element_type=F32)
         up = jnp.dot(nb[...], wu[...], preferred_element_type=F32)
         hb[...] = (gate / (1.0 + jnp.exp(-gate)) * up).astype(BF16)
+    def compute_out(c):
         term = jnp.dot(hb[...], wd[...], preferred_element_type=F32)
         for j in range(0, D, TILE):
             turned = term[:, j : j + TILE]
@@ -259,35 +258,34 @@
         rot[c, low:high, columns(yy, zz)] = total.astype(BF16)
 
     def sum_two(c):
-        arrive(c, 15, 16)
+        arrive(c, 6)
         add(c, 0, S_LO, yf, z, land1[c, 0:S_LO])
         add(c, S_HI, ROWS, yf, z, land1[c, S_HI:ROWS])
         start(c, 19, 20)
-        arrive(c, 17)
-        add(c, S_LO, HALF, yp, zb, land1[c, S_LO:HALF])
+        arrive(c, 7)
+        add(c, S_LO, S_HALF, yp, zb, land1[c, S_LO:S_HALF])
         start(c, 21)
-        arrive(c, 18)
-        add(c, HALF, S_HI, ym, zb, land1[c, HALF:S_HI])
+        add(c, S_HALF, S_HI, ym, zb, land1[c, S_HALF:S_HI])
         start(c, 22, 23, 24, 25, 26)
 
     def sum_three(c):
-        arrive(c, 19, 23, 24)
+        arrive(c, 8)
         add(c, 0, S_LO, yp, z, land2[c, 0:S_LO], land2[c, EDGES : EDGES + S_LO])
-        add(c, S_LO, HALF, yp, z, land2[c, S_LO:HALF])
+        add(c, S_LO, S_HALF, yp, z, land2[c, S_LO:S_HALF])
         add(c, S_HI, ROWS, yp, z, land2[c, EDGES + S_LO : EDGES + EDGE])
         start(c, 27)
-        arrive(c, 20, 25, 26)
+        arrive(c, 9)
         add(c, 0, S_LO, ym, z, land2[c, EDGES + EDGE : EDGES + EDGE + S_LO])
-        add(c, HALF, S_HI, ym, z, land2[c, HALF:S_HI])
+        add(c, S_HALF, S_HI, ym, z, land2[c, S_HALF:S_HI])
         add(c, S_HI, ROWS, ym, z, land2[c, S_HI:ROWS], land2[c, EDGES + EDGE + S_LO : EDGES + 2 * EDGE])
         start(c, 28)
-        arrive(c, 21, 22)
+        arrive(c, 10)
         add(c, S_LO, S_HI, y, zb, land2[c, ROWS : ROWS + MIDDLE], land2[c, ROWS + MIDDLE : EDGES])
         start(c, 29)
 
     def finish(c):
-        arrive(c, 27, 28, 29)
-        out_rows = pl.ds(pl.multiple_of(c * ROWS, ROWS), ROWS)
+        arrive(c, 11)
+        out_rows = chunk_rows(c)
         for j in range(PART // 128):
             cols = pl.ds(pl.multiple_of((y * 2 + z) * PART + j * 128, 128), 128)
             here = slice(j * 128, (j + 1) * 128)
@@ -302,6 +300,7 @@
             incoming = xg[c, :, cols].astype(F32)
             out_ref[out_rows, here] = (incoming + update * (1.0 / math.sqrt(128.0))).astype(BF16)
 
+
     def step(i, carry):
         def stage(lag, work):
             @pl.when(jnp.logical_and(i >= lag, i < lag + CHUNKS))
@@ -324,30 +323,30 @@
         def _():
             loads[1].wait()
             loads[2].wait()
-            for q in range(1, n_tp):
-                gain_copy(q).wait_recv()
+            all_gains.wait_recv()
 
         stage(3, compute)
         stage(4, sum_two)
+        stage(3, compute_out)
         stage(5, sum_three)
         stage(6, finish)
         return carry
 
     lax.fori_loop(0, CHUNKS + 6, step, 0)
 
-    def drain(c, carry):
-        for k in range(COPIES):
-            copy(c, k).wait_send()
-
-        @pl.when(has_next)
-        def _():
-            relay(c).wait_send()
-
-        return carry
-
-    lax.fori_loop(0, CHUNKS, drain, 0)
-    for q in range(1, n_tp):
-        gain_copy(q).wait_send()
+    sevenths = xg.at[:, :, pl.ds(0, (N_TP - 1) * PART)]
+    for phase in range(2):
+        pltpu.make_async_remote_copy(
+            sevenths, sevenths, sent.at[phase], gained, device_id=dev_z, device_id_type=MESH
+        ).wait_send()
+
+    @pl.when(has_next)
+    def _():
+        pltpu.make_async_remote_copy(
+            prev_ref, prev_ref, sent.at[2], gained, device_id=next_dev, device_id_type=MESH
+        ).wait_send()
+
+    all_gains.wait_send()
 
 
 def local(fresh_input, previous_out, norm_gain, gate_weight, up_weight, down_weight):
@@ -356,8 +355,8 @@
     dma = pltpu.SemaphoreType.DMA
     return pl.pallas_call(
         kernel,
-        out_shape=jax.ShapeDtypeStruct((TOK, PART), BF16),
-        in_specs=[anywhere, anywhere, vmem, anywhere, anywhere, anywhere],
+        out_shape=pltpu.VMEM((TOK, PART), BF16),
+        in_specs=[anywhere] * 6,
         out_specs=vmem,
         scratch_shapes=[
             pltpu.VMEM((CHUNKS, ROWS, D), BF16),
@@ -373,14 +372,13 @@
             pltpu.VMEM((8, D), F32),
             pltpu.VMEM((TILE, TILE), BF16),
             pltpu.VMEM((TILE, TILE), BF16),
+            pltpu.VMEM((1, PART), BF16),
+            dma(()),
             dma((3,)),
             dma((CHUNKS,)),
-            dma((CHUNKS,)),
-            dma((CHUNKS,)),
-            dma((7,)),
-            dma((7,)),
-            dma((CHUNKS, COPIES)),
-            dma((CHUNKS, COPIES)),
+            dma(()),
+            dma((4,)),
+            dma((CHUNKS, len(GROUPS))),
         ],
         compiler_params=pltpu.CompilerParams(
             collective_id=0, has_side_effects=True, vmem_limit_bytes=56 << 20

time: 97.9 us -> 90.7 us (0.926)
  Pallas kernels: 94.4 us -> 88.4 us
  local copies, waits for them, and re-layouts: 2.09 us -> 0.88 us
    pallas_call x1, Pallas kernels: 94.4 us -> 88.4 us  [local(): pl.pallas_call(kernel, out_shape=pltpu.VMEM((TOK, PART), BF16), in_specs=...]
    unnamed x1, local copies, waits for them, and re-layouts: 2.09 us -> 0.88 us
where the time goes in v4:
time: 90.7 us; the launch traced here: 89.3 us
  Pallas kernels  88.4 us (97%)
    pallas_call x1, Pallas kernels, local(): pl.pallas_call(kernel, out_shape=pltpu.VMEM((TOK, PART), BF16), in_specs=...  88.4 us

profile of v4, /device:TPU:0, one launch (start us, length us, event | category | flops | bytes accessed | tf_op | source)
XLA Modules:
  0.0 89.3 jit_solution(266114910604751759)
XLA Ops:
  0.0 88.4 %relayed_feed_forward.1 = bf16[1024,384]{1,0:T(8,128)(2,1)S(1)} custom-call(bf16[1024,384]{1,0:T(8,128)(2,1)} %fresh_ref.1, bf16[1024,384]{1,0:T(8,128)(2,1)} %prev_ref.1, bf16[1,384]{1,0:T(2,128)(2,1)} %gain_ref.1, bf16[1,3072,1024]{2,1,0:T(8,128)(2,1)} %gate_ref.1, bf16[1,3072,1024]{2,1,0:T(8,128)(2,1)} %up_ref.1, bf16[1,1024,3072]{2,1,0:T(8,128)(2,1)} %down_ref.1), custom_call_target="tpu_custom_call" | custom-call | flops 19327352832 | bytes 18874368 | tf_op jit(solution)/shard_map/relayed_feed_forward/pallas_call | solution.py:356
  88.4 0.9 copy.8

commit v5 on v4

--- a/solution.py
+++ b/solution.py
@@ -67,24 +67,39 @@
         pltpu.make_async_copy(src, dst, load_sem.at[i])
         for i, (src, dst) in enumerate(((down_ref.at[0], wd), (gate_ref.at[0], wg), (up_ref.at[0], wu)))
     ]
+    barrier = pltpu.get_barrier_semaphore()
+    for q in range(1, n_tp):
+        pl.semaphore_signal(barrier, inc=1, device_id=(s, (t + q) % n_tp), device_id_type=MESH)
+
+    around = (t, y * 2 + zb, yp * 2 + z, ym * 2 + z)
+
+    @pl.when(core == 0)
+    def _():
+        for at in around:
+            pl.semaphore_signal(barrier, inc=1, device_id=(s + 1, at), device_id_type=MESH)
+
+    @pl.when(core == 1)
+    def _():
+        for at in around:
+            pl.semaphore_signal(barrier, inc=1, device_id=(s - 1, at), device_id_type=MESH)
+
+    far_next = jnp.logical_and(core == 1, has_next)
+    far_prev = jnp.logical_and(core == 0, has_prev)
+
+    @pl.when(far_next)
+    def _():
+        pl.semaphore_signal(barrier, inc=1, device_id=next_dev, device_id_type=MESH)
+
+    @pl.when(far_prev)
+    def _():
+        pl.semaphore_signal(barrier, inc=1, device_id=prev_dev, device_id_type=MESH)
+
     gain_load = pltpu.make_async_copy(gain_ref, gain, gain_sem)
     gain_load.start()
     for load in loads:
         load.start()
 
-    barrier = pltpu.get_barrier_semaphore()
-    for q in range(1, n_tp):
-        pl.semaphore_signal(barrier, inc=1, device_id=(s, (t + q) % n_tp), device_id_type=MESH)
-
-    @pl.when(has_next)
-    def _():
-        pl.semaphore_signal(barrier, inc=1, device_id=next_dev, device_id_type=MESH)
-
-    @pl.when(has_prev)
-    def _():
-        pl.semaphore_signal(barrier, inc=1, device_id=prev_dev, device_id_type=MESH)
-
-    pl.semaphore_wait(barrier, n_tp - 1 + has_next.astype(jnp.int32) + has_prev.astype(jnp.int32))
+    pl.semaphore_wait(barrier, n_tp + 3 + far_next.astype(jnp.int32) + far_prev.astype(jnp.int32))
 
     def columns(yy, zz):
         return pl.ds(pl.multiple_of((yy * 2 + zz) * PART, 128), PART)
@@ -102,6 +117,18 @@
             device_id_type=MESH,
         )
 
+    @pl.when(core == 0)
+    def _():
+        for d in range(3):
+            pltpu.make_async_remote_copy(
+                prev_ref.at[pl.ds(0, ROWS)],
+                xg.at[0, :, columns(y, z)],
+                sent.at[2],
+                landed.at[0, d],
+                device_id=(s + 1, around[d + 1]),
+                device_id_type=MESH,
+            ).start()
+
     @pl.when(has_next)
     def _():
         for c in range(CHUNKS):
@@ -121,11 +148,6 @@
         )
 
     all_gains = gain_copy(pl.ds(0, (N_TP - 1) * PART), dev_z)
-
-    gain_load.wait()
-    gains[0:1, columns(y, z)] = gain[...].astype(F32)
-    for q in range(1, n_tp):
-        gain_copy(columns(y, z), (s, (t + q) % n_tp)).start()
 
     row_id = lax.broadcasted_iota(jnp.int32, (TILE, TILE), 0)
     col_id = lax.broadcasted_iota(jnp.int32, (TILE, TILE), 1)
@@ -187,7 +209,7 @@
     def copy(c, k):
         src, dst, dev = gathered(c, k) if k < 15 else summed(c, k)
         return pltpu.make_async_remote_copy(
-            src, dst, sent.at[k // 15], landed.at[c, GROUP_OF[k]], device_id=dev, device_id_type=MESH
+            src, dst, sent.at[4 if k < 3 else k // 15], landed.at[c, GROUP_OF[k]], device_id=dev, device_id_type=MESH
         )
 
     def start(c, *ks):
@@ -202,7 +224,10 @@
 
     def gather_one(c):
         relay(c).wait_recv()
-        start(c, 0, 1, 2)
+
+        @pl.when(jnp.logical_or(c > 0, core == 0))
+        def _():
+            start(c, 0, 1, 2)
 
     def gather_two(c):
         arrive(c, 1)
@@ -308,6 +333,14 @@
                 work(i - lag)
 
         stage(0, gather_one)
+
+        @pl.when(i == 0)
+        def _():
+            gain_load.wait()
+            gains[0:1, columns(y, z)] = gain[...].astype(F32)
+            for q in range(1, n_tp):
+                gain_copy(columns(y, z), (s, (t + q) % n_tp)).start()
+
         stage(1, gather_two)
         stage(2, gather_three)
 
@@ -334,17 +367,26 @@
 
     lax.fori_loop(0, CHUNKS + 6, step, 0)
 
-    sevenths = xg.at[:, :, pl.ds(0, (N_TP - 1) * PART)]
-    for phase in range(2):
+    def all_sent(ref, sem):
         pltpu.make_async_remote_copy(
-            sevenths, sevenths, sent.at[phase], gained, device_id=dev_z, device_id_type=MESH
+            ref, ref, sent.at[sem], gained, device_id=dev_z, device_id_type=MESH
         ).wait_send()
 
-    @pl.when(has_next)
-    def _():
-        pltpu.make_async_remote_copy(
-            prev_ref, prev_ref, sent.at[2], gained, device_id=next_dev, device_id_type=MESH
-        ).wait_send()
+    all_sent(xg.at[:, :, pl.ds(0, 4 * PART)], 0)
+    all_sent(xg.at[:, :, pl.ds(0, 7 * PART)], 1)
+
+    @pl.when(core == 0)
+    def _():
+        all_sent(xg.at[:, :, pl.ds(0, 3 * PART)], 4)
+        all_sent(xg.at[0, :, pl.ds(0, (CHUNKS + 3) * PART)], 2)
+
+    @pl.when(core == 1)
+    def _():
+        all_sent(xg.at[pl.ds(0, CHUNKS - 1), :, pl.ds(0, 3 * PART)], 4)
+
+    @pl.when(far_next)
+    def _():
+        all_sent(xg.at[0, :, pl.ds(0, CHUNKS * PART)], 2)
 
     all_gains.wait_send()
 
@@ -377,7 +419,7 @@
             dma((3,)),
             dma((CHUNKS,)),
             dma(()),
-            dma((4,)),
+            dma((5,)),
             dma((CHUNKS, len(GROUPS))),
         ],
         compiler_params=pltpu.CompilerParams(

time: 90.7 us -> 89.8 us (0.990); the launches traced: 89.3 us -> 89.7 us
  no operation moved by 1% of the time
where the time goes in v5:
time: 89.8 us; the launch traced here: 89.7 us
  Pallas kernels  88.8 us (99%)
    pallas_call x1, Pallas kernels, local(): pl.pallas_call(kernel, out_shape=pltpu.VMEM((TOK, PART), BF16), in_specs=...  88.8 us

profile of v5, /device:TPU:0, one launch (start us, length us, event | category | flops | bytes accessed | tf_op | source)
XLA Modules:
  0.0 89.7 jit_solution(10759224427764931993)
XLA Ops:
  0.0 88.8 %relayed_feed_forward.1 = bf16[1024,384]{1,0:T(8,128)(2,1)S(1)} custom-call(bf16[1024,384]{1,0:T(8,128)(2,1)} %fresh_ref.1, bf16[1024,384]{1,0:T(8,128)(2,1)} %prev_ref.1, bf16[1,384]{1,0:T(2,128)(2,1)} %gain_ref.1, bf16[1,3072,1024]{2,1,0:T(8,128)(2,1)} %gate_ref.1, bf16[1,3072,1024]{2,1,0:T(8,128)(2,1)} %up_ref.1, bf16[1,1024,3072]{2,1,0:T(8,128)(2,1)} %down_ref.1), custom_call_target="tpu_custom_call" | custom-call | flops 19327352832 | bytes 18874368 | tf_op jit(solution)/shard_map/relayed_feed_forward/pallas_call | solution.py:398
  88.8 0.9 copy.8

commit v6 on v5

--- a/solution.py
+++ b/solution.py
@@ -276,6 +276,10 @@
             rot[c, :, j : j + TILE] = jnp.minimum(jnp.maximum(turned, -limit), limit).astype(BF16)
         start(c, 15, 16, 17, 18)
 
+        @pl.when(c == CHUNKS - 1)
+        def _():
+            start(c, 23, 24, 25, 26)
+
     def add(c, low, high, yy, zz, *others):
         total = rot[c, low:high, columns(yy, zz)].astype(F32)
         for other in others:
@@ -291,7 +295,11 @@
         add(c, S_LO, S_HALF, yp, zb, land1[c, S_LO:S_HALF])
         start(c, 21)
         add(c, S_HALF, S_HI, ym, zb, land1[c, S_HALF:S_HI])
-        start(c, 22, 23, 24, 25, 26)
+        start(c, 22)
+
+        @pl.when(c < CHUNKS - 1)
+        def _():
+            start(c, 23, 24, 25, 26)
 
     def sum_three(c):
         arrive(c, 8)

time: 89.8 us -> 89.8 us (level)
  no operation moved by 1% of the time
where the time goes in v6:
time: 89.8 us; the launch traced here: 89.7 us
  Pallas kernels  88.8 us (99%)
    pallas_call x1, Pallas kernels, local(): pl.pallas_call(kernel, out_shape=pltpu.VMEM((TOK, PART), BF16), in_specs=...  88.8 us

profile of v6, /device:TPU:0, one launch (start us, length us, event | category | flops | bytes accessed | tf_op | source)
XLA Modules:
  0.0 89.7 jit_solution(2659785202152504685)
XLA Ops:
  0.0 88.8 %relayed_feed_forward.1 = bf16[1024,384]{1,0:T(8,128)(2,1)S(1)} custom-call(bf16[1024,384]{1,0:T(8,128)(2,1)} %fresh_ref.1, bf16[1024,384]{1,0:T(8,128)(2,1)} %prev_ref.1, bf16[1,384]{1,0:T(2,128)(2,1)} %gain_ref.1, bf16[1,3072,1024]{2,1,0:T(8,128)(2,1)} %gate_ref.1, bf16[1,3072,1024]{2,1,0:T(8,128)(2,1)} %up_ref.1, bf16[1,1024,3072]{2,1,0:T(8,128)(2,1)} %down_ref.1), custom_call_target="tpu_custom_call" | custom-call | flops 19327352832 | bytes 18874368 | tf_op jit(solution)/shard_map/relayed_feed_forward/pallas_call | solution.py:406
  88.8 0.9 copy.8
